TPU v7x, 768 devices: a whole 4x8x12 slice. The times are simulated.
768 devices in a mesh: dp: 48 (over x, z), heads: 16 (over y, core).
Axes of the slice: x: 4, y: 8, z: 12, core: 2. Of those that a mesh axis runs over, the one named last changes fastest.
Arguments:
- patch_queries: bfloat16 [49152, 6144], P('dp', 'heads'), may hold values from -144 to 144
- patch_keys: bfloat16 [49152, 6144], P('dp', 'heads'), may hold values from -6 to 6
- patch_values: bfloat16 [49152, 6144], P('dp', 'heads'), may hold values from -6 to 6
- out_proj: bfloat16 [6144, 6144], P('heads'), may hold values from -0.625 to 0.625
- pool_grad: bfloat16 [144, 6144], P('dp', 'heads'), may hold values from -6 to 6
- image_of_slot: int32 [49152], P('dp'), may hold values from -1 to 2, as said below
Outputs:
- pooled: bfloat16 [144, 6144], P('dp', 'heads')
- query_grad: bfloat16 [49152, 6144], P('dp', 'heads')
- key_grad: bfloat16 [49152, 6144], P('dp', 'heads')
- value_grad: bfloat16 [49152, 6144], P('dp', 'heads')
Inputs may be any that keep to these rules, and one draw needn't show every extreme that they name: `image_of_slot`: within a block, slot m * 256 + c (m < 1, c < 256) holds image m or -1, live slots a prefix of the 256; slot 256 + j * 384 + c (j < 2, c < 384) holds image 1 + j or -1, live slots a prefix of the 384. Only blocks of dp index below 24 hold live slots of images 1 and above; in each of them image 0 fills 256 slots, every image has live slots and image 1 fills 384; in some of them image 2 fills 384 as well.
All inputs are finite; a program needn't handle non-finite values.
Results may differ from a plain program's by a relative error of at most 0.023.
Values may be sent and summed in bfloat16 or wider, within the bound.
No kernel may reach another device: no remote copies, remote signals or barrier semaphores. Data moves between devices by JAX's collectives and lax.ppermute only.
A program may use at most 64 MiB of HBM per device.

v0:
```python
import jax
import jax.numpy as jnp
from jax import lax
from jax.sharding import PartitionSpec as P

HS = 128
STAY_LEN = 256
STAY_IMG = 1
MOVE_IMG = 2
CAP = 384


def passed_along(x, axis, by):
    peers = lax.axis_size(axis)
    pairs = [(i, i + by) for i in range(peers) if 0 <= i + by < peers]
    return lax.ppermute(x, axis, pairs)


def score_probs(query_heads, key_heads, segment):
    scores = jnp.einsum(
        "qhd,khd->hqk", query_heads, key_heads, preferred_element_type=jnp.float32
    ) * HS ** (-0.5)
    row_total = segment.shape[0]
    allowed = (segment[:, None] == segment[None, :]) & (segment[:, None] >= 0) | jnp.eye(
        row_total, dtype=bool
    )
    scores = jnp.where(allowed[None], scores, -1e30)
    scores = scores - jnp.max(scores, axis=-1, keepdims=True)
    weights = jnp.exp(scores)
    return weights / jnp.sum(weights, axis=-1, keepdims=True)


def forward_tile(block):
    query_tile, key_tile, value_tile, segment = block
    row_count = query_tile.shape[0]

    def forward_compute():
        query_heads = query_tile.reshape(row_count, -1, HS)
        key_heads = key_tile.reshape(row_count, -1, HS)
        value_heads = value_tile.reshape(row_count, -1, HS)
        weights = score_probs(query_heads, key_heads, segment).astype(jnp.bfloat16)
        attended = jnp.einsum(
            "hqk,khd->qhd", weights, value_heads, preferred_element_type=jnp.float32
        )
        return attended.astype(jnp.bfloat16).reshape(row_count, -1)

    def forward_skipped():
        return jnp.zeros_like(query_tile)

    return lax.cond(jnp.any(segment >= 0), forward_compute, forward_skipped)


def backward_tile(block):
    query_tile, key_tile, value_tile, segment, grad_tile = block
    row_count = query_tile.shape[0]

    def backward_compute():
        query_heads = query_tile.reshape(row_count, -1, HS)
        key_heads = key_tile.reshape(row_count, -1, HS)
        value_heads = value_tile.reshape(row_count, -1, HS)
        grad_heads = grad_tile.reshape(row_count, -1, HS)
        prob = score_probs(query_heads, key_heads, segment)
        weights = prob.astype(jnp.bfloat16)
        value_grad = jnp.einsum(
            "hqk,qhd->khd", weights, grad_heads, preferred_element_type=jnp.float32
        )
        prob_grad = jnp.einsum(
            "qhd,khd->hqk", grad_heads, value_heads, preferred_element_type=jnp.float32
        )
        delta = jnp.sum(prob * prob_grad, axis=-1, keepdims=True)
        score_grad = (prob * (prob_grad - delta) * HS ** (-0.5)).astype(jnp.bfloat16)
        query_grad = jnp.einsum(
            "hqk,khd->qhd", score_grad, key_heads, preferred_element_type=jnp.float32
        )
        key_grad = jnp.einsum(
            "hqk,qhd->khd", score_grad, query_heads, preferred_element_type=jnp.float32
        )
        return (
            query_grad.astype(jnp.bfloat16).reshape(row_count, -1),
            key_grad.astype(jnp.bfloat16).reshape(row_count, -1),
            value_grad.astype(jnp.bfloat16).reshape(row_count, -1),
        )

    def backward_skipped():
        return (jnp.zeros_like(query_tile), jnp.zeros_like(query_tile), jnp.zeros_like(query_tile))

    return lax.cond(jnp.any(segment >= 0), backward_compute, backward_skipped)


def by_tiles(worker, arrays, row_count):
    tile_count = arrays[0].shape[0] // row_count
    shaped = tuple((array.reshape((tile_count, row_count) + array.shape[1:]) for array in arrays))
    result = lax.map(worker, shaped)
    return jax.tree.map(
        lambda array: array.reshape((tile_count * row_count,) + array.shape[2:]), result
    )


def attend(worker, arrays):
    stay_rows = STAY_IMG * STAY_LEN
    front = by_tiles(worker, tuple((array[:stay_rows] for array in arrays)), STAY_LEN)
    back = by_tiles(worker, tuple((array[stay_rows:] for array in arrays)), CAP)
    return jax.tree.map(lambda first, second: jnp.concatenate([first, second], axis=0), front, back)


def image_members(segment, image_count):
    image_ids = jnp.arange(image_count, dtype=jnp.int32)
    member = segment[None, :] == image_ids[:, None]
    counts = jnp.sum(member.astype(jnp.float32), axis=1)
    return (member.astype(jnp.bfloat16), jnp.maximum(counts, 1.0)[:, None])


def token_grads(grad_rows, member, divisor, out_proj):
    summed = lax.dot_general(
        lax.all_gather(grad_rows, "heads", axis=1, tiled=True),
        out_proj,
        (((1,), (1,)), ((), ())),
        preferred_element_type=jnp.float32,
    )
    image_grad = (summed / divisor).astype(jnp.bfloat16)
    spread = lax.dot_general(
        member, image_grad, (((0,), (0,)), ((), ())), preferred_element_type=jnp.float32
    )
    return spread.astype(jnp.bfloat16)


def pool_images(attended, member, divisor, out_proj):
    mean = (jnp.dot(member, attended, preferred_element_type=jnp.float32) / divisor).astype(
        jnp.bfloat16
    )
    partial_sum = jnp.dot(mean, out_proj, preferred_element_type=jnp.float32)
    return lax.psum_scatter(
        partial_sum.astype(jnp.bfloat16), "heads", scatter_dimension=1, tiled=True
    )


def on_device(patch_queries, patch_keys, patch_values, out_proj, pool_grad, image_of_slot):
    stay_rows = STAY_IMG * STAY_LEN
    image_total = pool_grad.shape[0]
    dp_count = lax.axis_size("dp")
    half_count = dp_count // 2
    my_index = lax.axis_index("dp")
    busy = my_index < half_count
    keep_img = MOVE_IMG // 2
    keep_end = stay_rows + keep_img * CAP
    send_slots = (MOVE_IMG - keep_img) * CAP
    col_width = patch_queries.shape[1]
    packed = jnp.concatenate([patch_queries, patch_keys, patch_values], axis=1)
    send_rows = packed[keep_end:]
    send_live = (image_of_slot[keep_end:] >= 0).astype(jnp.bfloat16)
    send_grad = pool_grad[STAY_IMG + keep_img :]
    got_rows, got_live, got_grad = passed_along((send_rows, send_live, send_grad), "dp", half_count)
    slot_image = STAY_IMG + keep_img + jnp.arange(send_slots, dtype=jnp.int32) // CAP
    moved_segment = jnp.where(got_live > 0, slot_image, -1)
    work_moving = jnp.where(busy, packed[stay_rows:keep_end], got_rows)
    work_rows = jnp.concatenate([packed[:stay_rows], work_moving], axis=0)
    work_segment = jnp.concatenate(
        [
            image_of_slot[:stay_rows],
            jnp.where(busy, image_of_slot[stay_rows:keep_end], moved_segment),
        ],
        axis=0,
    )
    work_grad_rows = jnp.concatenate([pool_grad[: STAY_IMG + keep_img], got_grad], axis=0)
    member, divisor = image_members(work_segment, image_total)
    out_grad = token_grads(work_grad_rows, member, divisor, out_proj)
    arrays = (
        work_rows[:, :col_width],
        work_rows[:, col_width : 2 * col_width],
        work_rows[:, 2 * col_width :],
        work_segment,
    )
    attended = attend(forward_tile, arrays)
    pooled_work = pool_images(attended, member, divisor, out_proj)
    back_pooled = pooled_work[STAY_IMG + keep_img :]
    home_pooled = passed_along(back_pooled, "dp", -half_count)
    grads = attend(backward_tile, arrays + (out_grad,))
    all_work = jnp.concatenate(grads, axis=1)
    home_grads = passed_along(all_work[stay_rows:], "dp", -half_count)
    pooled = jnp.concatenate([pooled_work[: STAY_IMG + keep_img], home_pooled], axis=0)
    kept_grads = jnp.where(busy, all_work[stay_rows:], 0)
    all_grads = jnp.concatenate([all_work[:stay_rows], kept_grads, home_grads], axis=0)
    return (
        pooled,
        all_grads[:, :col_width],
        all_grads[:, col_width : 2 * col_width],
        all_grads[:, 2 * col_width :],
    )


def solution(mesh):
    in_specs = (
        P("dp", "heads"),
        P("dp", "heads"),
        P("dp", "heads"),
        P("heads", None),
        P("dp", "heads"),
        P("dp"),
    )
    out_specs = (P("dp", "heads"), P("dp", "heads"), P("dp", "heads"), P("dp", "heads"))
    return jax.shard_map(
        on_device, mesh=mesh, in_specs=in_specs, out_specs=out_specs, check_vma=False
    )
```

profile of v0, /device:TPU:1, one launch (start us, length us, event | category | flops | bytes accessed | tf_op | source)
XLA Modules:
  0.0 204.3 jit_solution(15603467477426371942)
XLA Ops:
  8.0 5.5 %collective-permute-start = (bf16[384]{0:T(512)(128)(2,1)S(1)}, bf16[384]{0:T(512)(128)(2,1)S(1)}, u32[]{:S(2)}, u32[]{:S(2)}) collective-permute-start(bf16[384]{0:T(512)(128)(2,1)S(1)} %fusion.105), channel_id=1, source_target_pairs={{0,384},{16,400},{32,416},{48,432},{64,448},{80,464},{96,480},{112... | collective-permute-start | bytes 2312 | tf_op jit(solution)/shard_map/ppermute | solution.py:16
  13.5 1.2 constant_dynamic-update-slice_fusion.2
  15.2 1.0 slice.120
  16.2 2.2 %collective-permute-start.1 = (bf16[384,1152]{1,0:T(8,128)(2,1)}, bf16[384,1152]{1,0:T(8,128)(2,1)}, u32[]{:S(2)}, u32[]{:S(2)}) collective-permute-start(bf16[384,1152]{1,0:T(8,128)(2,1)} %slice.120), channel_id=1, source_target_pairs={{0,384},{16,400},{32,416},{48,432},{64,448},{80,464},{96,480},{112... | collective-permute-start | bytes 2654216 | tf_op jit(solution)/shard_map/ppermute | solution.py:16
  18.4 1.3 collective-permute-start.3
  21.0 0.8 copy.189
  21.8 0.8 copy.190
  24.7 5.9 %collective-permute-done.3 = bf16[1,384]{1,0:T(2,128)(2,1)S(1)} collective-permute-done((bf16[1,384]{1,0:T(2,128)(2,1)S(1)}, bf16[1,384]{1,0:T(2,128)(2,1)S(1)}, u32[]{:S(2)}, u32[]{:S(2)}) %collective-permute-start.3) | collective-permute-done | bytes 800 | tf_op jit(solution)/shard_map/ppermute | solution.py:16
  30.7 24.5 %all_gather.3 = bf16[3,6144]{1,0:T(4,128)(2,1)S(1)} all-gather(bf16[3,384]{1,0:T(4,128)(2,1)S(1)} %pad_maximum_fusion.4), channel_id=1, replica_groups=mesh['dp'=48,'heads'=16] {'heads'}, dimensions={1}, use_global_device_ids=true | all-gather | bytes 39168 | tf_op jit(solution)/shard_map/all_gather | solution.py:115
  55.3 4.2 %convolution_convert_fusion.7 = bf16[640,384]{1,0:T(8,128)(2,1)S(1)} fusion(bf16[3,6144]{1,0:T(4,128)(2,1)S(1)} %all_gather.3, bf16[384,6144]{1,0:T(8,128)(2,1)} %param.17, s32[640]{0:T(1024)S(1)} %pad_add_fusion, f32[3]{0:T(128)S(1)} %broadcast_maximum_fusion), kind=kOutput, calls=%fused_computation.100 | convolution fusion | flops 15880320 | bytes 5249548 | tf_op jit(solution)/shard_map/dot_general | solution.py:121
  59.5 15.5 %conditional.6 = (bf16[256,384]{1,0:T(8,128)(2,1)S(1)}, bf16[256,384]{1,0:T(8,128)(2,1)S(1)}, bf16[256,384]{1,0:T(8,128)(2,1)S(1)}) conditional(s32[]{:T(128)} %convert_element_type.100, () %tuple.48, (s32[256]{0:T(256)S(1)}, bf16[256,384]{0,1:T(8,128)(2,1)}, bf16[256,384]{0,1:T(8,128)(2,1)}, bf16[640,384]{1,0:T(8,128)(2,1)S(1)}, ...), branch_computations={%region_12.13_spmd, %region_13.17_spmd} | conditional | flops 307072512 | bytes 12204652 | solution.py:87
  60.5 2.1 %fusion.116 = f32[3,256,256]{1,2,0:T(8,128)} fusion(bf16[256,3,128]{0,2,1:T(8,128)(2,1)S(1)} %bitcast.87, bf16[256,3,128]{0,2,1:T(8,128)(2,1)} %bitcast.85), kind=kOutput, calls=%fused_computation.148 | convolution fusion | flops 50331648 | bytes 1179648 | tf_op jit(solution)/shard_map/while/body/eval_jaxpr/cond/branch_1_fun/qhd,khd->hqk/dot_general | solution.py:67
  62.7 2.2 %fusion.112 = (f32[3,256]{1,0:T(4,128)S(1)}, f32[3,256,256]{1,2,0:T(8,128)}) fusion(bf16[256,3,128]{0,2,1:T(8,128)(2,1)S(1)} %bitcast.75, bf16[256,3,128]{0,2,1:T(8,128)(2,1)} %bitcast.80, pred[256,256]{0,1:T(8,128)(4,1)S(1)} %fusion.34), kind=kOutput, calls=%fused_computation.144 | convolution fusion | flops 51118336 | bytes 1248256 | tf_op jit(solution)/shard_map/while/body/eval_jaxpr/cond/branch_1_fun/sub | solution.py:28
  65.0 2.3 %convolution_convert_fusion.2 = bf16[3,256,128]{1,2,0:T(8,128)(2,1)S(1)} fusion(bf16[256,3,128]{0,2,1:T(8,128)(2,1)S(1)} %bitcast.82, f32[3,256,256]{1,2,0:T(8,128)} %fusion.116, f32[3,256,256]{1,2,0:T(8,128)} %get-tuple-element.238, f32[3,256]{1,0:T(4,128)S(1)} %get-tuple-element.237), kind=kOutput, calls=%fused_computation.38 | convolution fusion | flops 51807232 | bytes 1969152 | tf_op jit(solution)/shard_map/while/body/eval_jaxpr/cond/branch_1_fun/hqk,khd->qhd/dot_general | solution.py:72
  67.5 3.0 %convolution_convert_fusion.4 = bf16[3,256,128]{1,2,0:T(8,128)(2,1)} fusion(bf16[256,3,128]{0,2,1:T(8,128)(2,1)S(1)} %bitcast.76, f32[3,256,256]{1,2,0:T(8,128)} %fusion.116, f32[3,256,256]{1,2,0:T(8,128)} %get-tuple-element.238, f32[3,256]{1,0:T(4,128)S(1)} %get-tuple-element.237), kind=kOutput, calls=%fused_computation.40 | convolution fusion | flops 51807232 | bytes 1969152 | tf_op jit(solution)/shard_map/while/body/eval_jaxpr/cond/branch_1_fun/hqk,qhd->khd/dot_general | solution.py:75
  70.5 1.1 copy.180
  71.6 2.3 %convolution_convert_fusion.3 = bf16[3,256,128]{1,2,0:T(8,128)(2,1)} fusion(bf16[256,3,128]{0,2,1:T(8,128)(2,1)} %bitcast.88, f32[3,256]{1,0:T(4,128)S(1)} %get-tuple-element.237, bf16[256,3,128]{0,2,1:T(8,128)(2,1)S(1)} %bitcast.77, bf16[256,3,128]{0,2,1:T(8,128)(2,1)} %bitcast.81, pred[256,256]{0,1:T(8,128)(4,1)S(1)} %fusion.34), kind=kOutput, calls=%fused_computation.39 | convolution fusion | flops 101745664 | bytes 855040 | tf_op jit(solution)/shard_map/while/body/eval_jaxpr/cond/branch_1_fun/hqk,qhd->khd/dot_general | solution.py:64
  73.9 1.1 copy.182
  75.3 19.6 %conditional.7 = (bf16[384,384]{1,0:T(8,128)(2,1)S(1)}, bf16[384,384]{1,0:T(8,128)(2,1)S(1)}, bf16[384,384]{1,0:T(8,128)(2,1)S(1)}) conditional(s32[]{:T(128)} %convert_element_type.101, () %tuple.50, (s32[384]{0:T(512)S(1)}, bf16[384,384]{1,0:T(8,128)(2,1)S(1)}, bf16[384,384]{1,0:T(8,128)(2,1)S(1)}, bf16[640,384]{1,0:T(8,128)(2,1)S(1)}, ...), branch_computations={%region_17.18_spmd, %region_18.22_spmd} | conditional | flops 576114432 | bytes 29022032 | solution.py:87
  75.3 0.9 copy.146
  77.2 0.9 copy.148
  78.1 1.5 fusion.117
  79.8 1.1 copy.145
  80.9 3.1 %fusion.113 = (f32[3,384]{1,0:T(4,128)S(1)}, f32[3,384,384]{1,2,0:T(8,128)}) fusion(pred[384,384]{0,1:T(8,128)(4,1)S(1)} %fusion.66, bf16[384,3,128]{0,2,1:T(8,128)(2,1)} %bitcast.94, bf16[384,3,128]{0,2,1:T(8,128)(2,1)} %bitcast.91), kind=kOutput, calls=%fused_computation.145 | convolution fusion | flops 115016064 | bytes 2511360 | tf_op jit(solution)/shard_map/while/body/eval_jaxpr/cond/branch_1_fun/sub | solution.py:28
  83.9 3.4 %fusion.54 = bf16[3,384,128]{1,2,0:T(8,128)(2,1)} fusion(bf16[384,3,128]{0,2,1:T(8,128)(2,1)} %bitcast.92, f32[3,384,384]{1,2,0:T(8,128)S(1)} %fusion.117, f32[3,384,384]{1,2,0:T(8,128)} %get-tuple-element.240, f32[3,384]{1,0:T(4,128)S(1)} %get-tuple-element.239), kind=kOutput, calls=%fused_computation.68 | convolution fusion | flops 116491776 | bytes 4133376 | tf_op jit(solution)/shard_map/while/body/eval_jaxpr/cond/branch_1_fun/hqk,khd->qhd/dot_general | solution.py:72
  87.4 1.2 copy.184
  88.6 3.9 %fusion.57 = bf16[3,384,128]{1,2,0:T(8,128)(2,1)S(1)} fusion(bf16[384,3,128]{0,2,1:T(8,128)(2,1)} %bitcast.95, f32[3,384,384]{1,2,0:T(8,128)} %copy-done, f32[3,384,384]{1,2,0:T(8,128)} %get-tuple-element.240, f32[3,384]{1,0:T(4,128)S(1)} %get-tuple-element.239), kind=kOutput, calls=%fused_computation.69 | convolution fusion | flops 116491776 | bytes 4133376 | tf_op jit(solution)/shard_map/while/body/eval_jaxpr/cond/branch_1_fun/hqk,qhd->khd/dot_general | solution.py:75
  92.7 1.9 convolution_convert_fusion.5
  94.9 1.1 broadcast_select_fusion
  96.0 1.3 collective-permute-start.4
  97.3 5.6 %conditional.4 = (bf16[256,384]{0,1:T(8,128)(2,1)S(1)}) conditional(s32[]{:T(128)} %convert_element_type.100, () %tuple.44, (s32[256]{0:T(256)S(1)}, bf16[256,384]{0,1:T(8,128)(2,1)}, bf16[256,384]{0,1:T(8,128)(2,1)}, bf16[256,384]{0,1:T(8,128)(2,1)}) %tuple.45), branch_computations={%region_1.2_spmd, %region_2.5_spmd} | conditional | flops 153126400 | bytes 3744292 | solution.py:50
  97.4 1.5 fusion.110
  98.9 2.1 %fusion.3 = f32[3,256,256]{1,2,0:T(8,128)} fusion(bf16[256,3,128]{0,2,1:T(8,128)(2,1)S(1)} %bitcast.79, bf16[256,3,128]{0,2,1:T(8,128)(2,1)} %bitcast.84, pred[256,256]{0,1:T(8,128)(4,1)S(1)} %fusion.4), kind=kOutput, calls=%fused_computation.4 | convolution fusion | flops 50724864 | bytes 1245184 | tf_op jit(solution)/shard_map/while/body/eval_jaxpr/cond/branch_1_fun/qhd,khd->hqk/dot_general | solution.py:20
  101.0 1.8 convolution_convert_fusion
  102.8 7.2 %conditional.5 = (bf16[384,384]{0,1:T(8,128)(2,1)S(1)}) conditional(s32[]{:T(128)} %convert_element_type.101, () %tuple.46, (s32[384]{0:T(512)S(1)}, bf16[384,384]{1,0:T(8,128)(2,1)S(1)}, bf16[384,384]{1,0:T(8,128)(2,1)S(1)}, bf16[384,384]{1,0:T(8,128)(2,1)S(1)}) %tuple.47), branch_computations={%region_6.7_spmd, %region_7.10_spmd} | conditional | flops 229884672 | bytes 7975716 | solution.py:50
  103.0 0.9 copy.143
  103.9 0.8 fusion.13
  105.2 3.0 %fusion.111 = (f32[3,384]{1,0:T(4,128)S(1)}, f32[3,384,384]{1,2,0:T(8,128)}) fusion(pred[384,384]{0,1:T(8,128)(4,1)} %fusion.13, bf16[384,3,128]{0,2,1:T(8,128)(2,1)S(1)} %bitcast.96, bf16[384,3,128]{0,2,1:T(8,128)(2,1)S(1)} %bitcast.97), kind=kOutput, calls=%fused_computation.143 | convolution fusion | flops 115016064 | bytes 2511360 | tf_op jit(solution)/shard_map/while/body/eval_jaxpr/cond/branch_1_fun/sub | solution.py:28
  108.2 1.8 convolution_convert_fusion.1
  110.0 3.3 %convolution_convert_fusion.6 = bf16[3,6144]{1,0:T(4,128)(2,1)S(1)} fusion(bf16[384,6144]{1,0:T(8,128)(2,1)} %param.17, bf16[384,384]{0,1:T(8,128)(2,1)S(1)} %get-tuple-element.260, bf16[256,384]{0,1:T(8,128)(2,1)S(1)} %get-tuple-element.259, s32[640]{0:T(1024)S(1)} %pad_add_fusion, f32[3]{0:T(128)S(1)} %broadcast_maximum_fusion), kind=kOutput, calls=%fused_computation.88 | convolution fusion | flops 16636032 | bytes 5249548 | tf_op jit(solution)/shard_map/dot_general | solution.py:131
  113.4 1.6 copy.175
  115.0 69.0 %reduce-scatter.4.cloned.1.call-done = bf16[384,3]{1,0:T(8,128)(2,1)} async-done(((bf16[6144,3]{1,0:T(8,128)(2,1)}), bf16[384,3]{1,0:T(8,128)(2,1)}) %reduce-scatter.4.cloned.1.call-update) | async-done | bytes 2320
  184.0 1.0 slice.125
  185.1 1.3 collective-permute-start.2
  186.4 1.0 copy.192
  187.4 3.6 %collective-permute-done.2 = bf16[1,384]{1,0:T(2,128)(2,1)S(1)} collective-permute-done((bf16[1,384]{1,0:T(2,128)(2,1)S(1)}, bf16[1,384]{1,0:T(2,128)(2,1)S(1)}, u32[]{:S(2)}, u32[]{:S(2)}) %collective-permute-start.2) | collective-permute-done | bytes 800 | tf_op jit(solution)/shard_map/ppermute | solution.py:16
  191.6 4.4 %fusion.82 = bf16[1024,1152]{1,0:T(8,128)(2,1)S(1)} fusion(bf16[384,384]{1,0:T(8,128)(2,1)S(1)} %get-tuple-element.230, bf16[256,384]{1,0:T(8,128)(2,1)S(1)} %get-tuple-element.227, bf16[384,384]{1,0:T(8,128)(2,1)S(1)} %get-tuple-element.229, bf16[256,384]{1,0:T(8,128)(2,1)S(1)} %get-tuple-element.226, bf16[384,384]{1,0:T(8,128)(2,1)S(1)} %get-tuple-element.228, ...), kind=kLoop, calls=%fused_computation.97 | loop fusion | flops 23592960 | bytes 5603328 | tf_op jit(solution)/shard_map/concatenate | solution.py:182
  196.0 1.5 fusion.114
  (67 shorter events, 7.8 us)
Async XLA Ops:
  7.2 176.9 %reduce-scatter.4.cloned.1.call-start = ((), (), s32[]{:S(2)}) async-start(), calls=%async_computation.1 | async-start | bytes 1671168
  7.2 7.5 %copy-start.1 = (bf16[1024,384]{1,0:T(8,128)(2,1)S(1)}, bf16[1024,384]{1,0:T(8,128)(2,1)}, u32[]{:S(2)}) copy-start(bf16[1024,384]{1,0:T(8,128)(2,1)} %param.15) | copy-start | bytes 2359300
  7.2 7.7 %copy-start.2 = (bf16[1024,384]{1,0:T(8,128)(2,1)S(1)}, bf16[1024,384]{1,0:T(8,128)(2,1)}, u32[]{:S(2)}) copy-start(bf16[1024,384]{1,0:T(8,128)(2,1)} %param.16) | copy-start | bytes 2359300
  8.0 15.4 %collective-permute-start = (bf16[384]{0:T(512)(128)(2,1)S(1)}, bf16[384]{0:T(512)(128)(2,1)S(1)}, u32[]{:S(2)}, u32[]{:S(2)}) collective-permute-start(bf16[384]{0:T(512)(128)(2,1)S(1)} %fusion.105), channel_id=1, source_target_pairs={{0,384},{16,400},{32,416},{48,432},{64,448},{80,464},{96,480},{112... | collective-permute-start | bytes 2312 | tf_op jit(solution)/shard_map/ppermute | solution.py:16
  14.9 3.5 %copy-start.10 = (bf16[3,384]{1,0:T(4,128)(2,1)S(1)}, bf16[3,384]{1,0:T(4,128)(2,1)}, u32[]{:S(2)}) copy-start(bf16[3,384]{1,0:T(4,128)(2,1)} %param.18) | copy-start | bytes 6916
  14.9 4.8 %copy-start.9 = (s32[1024]{0:T(1024)S(1)}, s32[1024]{0:T(1024)}, u32[]{:S(2)}) copy-start(s32[1024]{0:T(1024)} %param.19) | copy-start | bytes 12292
  15.1 5.9 %slice-start = ((bf16[1024,384]{1,0:T(8,128)(2,1)}), bf16[256,384]{1,0:T(8,128)(2,1)S(1)}, s32[]{:S(2)}) async-start(bf16[1024,384]{1,0:T(8,128)(2,1)} %param.14), calls=%async_computation.2 | async-start | bytes 393216 | tf_op jit(solution)/shard_map/slice | solution.py:101
  15.1 6.7 %slice-start.1 = ((bf16[1024,384]{1,0:T(8,128)(2,1)}), bf16[256,384]{1,0:T(8,128)(2,1)S(1)}, s32[]{:S(2)}) async-start(bf16[1024,384]{1,0:T(8,128)(2,1)} %param.15), calls=%async_computation.3 | async-start | bytes 393216 | tf_op jit(solution)/shard_map/slice | solution.py:101
  15.1 7.5 %slice-start.2 = ((bf16[1024,384]{1,0:T(8,128)(2,1)}), bf16[256,384]{1,0:T(8,128)(2,1)S(1)}, s32[]{:S(2)}) async-start(bf16[1024,384]{1,0:T(8,128)(2,1)} %param.16), calls=%async_computation.4 | async-start | bytes 393216 | tf_op jit(solution)/shard_map/slice | solution.py:101
  15.2 15.5 %slice-start.3 = ((bf16[3,384]{1,0:T(4,128)(2,1)}), bf16[2,384]{1,0:T(2,128)(2,1)S(1)}, s32[]{:S(2)}) async-start(bf16[3,384]{1,0:T(4,128)(2,1)} %param.18), calls=%async_computation.5 | async-start | bytes 3072 | tf_op jit(solution)/shard_map/slice | solution.py:164
  16.2 58.9 %collective-permute-start.1 = (bf16[384,1152]{1,0:T(8,128)(2,1)}, bf16[384,1152]{1,0:T(8,128)(2,1)}, u32[]{:S(2)}, u32[]{:S(2)}) collective-permute-start(bf16[384,1152]{1,0:T(8,128)(2,1)} %slice.120), channel_id=1, source_target_pairs={{0,384},{16,400},{32,416},{48,432},{64,448},{80,464},{96,480},{112... | collective-permute-start | bytes 2654216 | tf_op jit(solution)/shard_map/ppermute | solution.py:16
  18.4 12.3 %collective-permute-start.3 = (bf16[1,384]{1,0:T(2,128)(2,1)S(1)}, bf16[1,384]{1,0:T(2,128)(2,1)S(1)}, u32[]{:S(2)}, u32[]{:S(2)}) collective-permute-start(bf16[1,384]{1,0:T(2,128)(2,1)S(1)} %slice.111), channel_id=1, source_target_pairs={{0,384},{16,400},{32,416},{48,432},{64,448},{80,464},{96,480},{112... | collective-permute-start | bytes 2312 | tf_op jit(solution)/shard_map/ppermute | solution.py:16
  59.5 3.2 %copy-start.4 = (bf16[256,384]{0,1:T(8,128)(2,1)S(1)}, bf16[256,384]{0,1:T(8,128)(2,1)}, u32[]{:S(2)}) copy-start(bf16[256,384]{0,1:T(8,128)(2,1)} %get-tuple-element.122) | copy-start | bytes 589828 | tf_op jit(solution)/shard_map/while/body/eval_jaxpr/cond
  59.8 0.7 copy-start.7
  59.8 5.2 %copy-start.6 = (bf16[256,384]{0,1:T(8,128)(2,1)S(1)}, bf16[256,384]{0,1:T(8,128)(2,1)}, u32[]{:S(2)}) copy-start(bf16[256,384]{0,1:T(8,128)(2,1)} %get-tuple-element.123) | copy-start | bytes 589828 | tf_op jit(solution)/shard_map/while/body/eval_jaxpr/cond
  79.6 7.8 %copy-start = (f32[3,384,384]{1,2,0:T(8,128)}, f32[3,384,384]{1,2,0:T(8,128)S(1)}, u32[]{:S(2)}) copy-start(f32[3,384,384]{1,2,0:T(8,128)S(1)} %fusion.117) | copy-start | bytes 5308420 | tf_op jit(solution)/shard_map/while/body/eval_jaxpr/cond
  88.6 4.2 %copy-start.3 = (bf16[384,384]{0,1:T(8,128)(2,1)S(1)}, bf16[384,384]{0,1:T(8,128)(2,1)}, u32[]{:S(2)}) copy-start(bf16[384,384]{0,1:T(8,128)(2,1)} %slice.118) | copy-start | bytes 884740 | tf_op jit(solution)/shard_map/while/body/eval_jaxpr/cond
  96.0 95.6 %collective-permute-start.4 = (bf16[384,1152]{1,0:T(8,128)(2,1)}, bf16[384,1152]{1,0:T(8,128)(2,1)}, u32[]{:S(2)}, u32[]{:S(2)}) collective-permute-start(bf16[384,1152]{1,0:T(8,128)(2,1)} %get-tuple-element.232), channel_id=1, source_target_pairs={{384,0},{400,16},{416,32},{432,48},{448,64},{464,80},{480,96},{496... | collective-permute-start | bytes 2654216 | tf_op jit(solution)/shard_map/ppermute | solution.py:16
  97.3 1.6 copy-start.5
  105.2 3.0 %copy-start.8 = (bf16[384,384]{0,1:T(8,128)(2,1)S(1)}, bf16[384,384]{0,1:T(8,128)(2,1)}, u32[]{:S(2)}) copy-start(bf16[384,384]{0,1:T(8,128)(2,1)} %copy.143) | copy-start | bytes 884740 | tf_op jit(solution)/shard_map/while/body/eval_jaxpr/cond
  185.1 5.8 %collective-permute-start.2 = (bf16[1,384]{1,0:T(2,128)(2,1)S(1)}, bf16[1,384]{1,0:T(2,128)(2,1)S(1)}, u32[]{:S(2)}, u32[]{:S(2)}) collective-permute-start(bf16[1,384]{1,0:T(2,128)(2,1)S(1)} %copy.193), channel_id=1, source_target_pairs={{384,0},{400,16},{416,32},{432,48},{448,64},{464,80},{480,96},{496... | collective-permute-start | bytes 2312 | tf_op jit(solution)/shard_map/ppermute | solution.py:16
Sparse Core Ops, SparseCore 0:
  115.1 68.8 reduce-scatter.3
where the time goes:
time: 206 us; the launch traced here: 204 us
  waiting for transfers between devices  78.6 us (38%)
  matrix products  43.6 us (21%)
  blocking collectives  24.5 us (12%)
  local copies, waits for them, and re-layouts  20.3 us (10%)
  between operations  15.6 us (8%)
  starting transfers between devices  11.6 us (6%)
  other arithmetic  9.74 us (5%)
    unnamed x2, waiting for transfers between devices  69.1 us
    all_gather x1, blocking collectives, token_grads(): lax.all_gather(grad_rows, 'heads', axis=1, tiled=True)  24.5 us
    ppermute x5, starting transfers between devices, passed_along(): return lax.ppermute(x, axis, pairs)  11.6 us
    sub x4, matrix products, score_probs(): scores = scores - jnp.max(scores, axis=-1, keepdims=True)  9.76 us
    ppermute x5, waiting for transfers between devices, passed_along(): return lax.ppermute(x, axis, pairs)  9.49 us
    dot_general x2, matrix products, backward_compute(): jnp.einsum('hqk,qhd->khd', score_grad, query_heads, preferred_element_typ...  6.95 us
    unnamed x16, local copies, waits for them, and re-layouts  6.5 us
    dot_general x2, matrix products, backward_compute(): jnp.einsum('hqk,khd->qhd', score_grad, key_heads, preferred_element_type=...  5.76 us
  transfers between devices with their start and end apart: 6, of which 3 were waited for; matrix products, arithmetic and copies ran while one was open for 22% of the time, Pallas kernels for 0%

commit v1 on v0

v1 whole, which is shorter than its diff:
```python
import functools

import jax
import jax.numpy as jnp
from jax import lax
from jax.experimental import pallas as pl
from jax.experimental.pallas import tpu as pltpu
from jax.sharding import PartitionSpec as P

HS = 128
D = 6144
HEADS_DEV = 3
WIDTH = HEADS_DEV * HS
PEERS = 16
SLOTS = 1024
IMG_DEV = 3
STARTS = (0, 256, 640)
SIZES = (256, 384, 384)
SCALE = HS**-0.5
LOG2E = 1.4426950408889634
ROWS = 8
VMEM_LIMIT = 24 * 2**20

NT = (((1,), (1,)), ((), ()))
NN = (((1,), (0,)), ((), ()))
TN = (((0,), (0,)), ((), ()))


def dot(a, b, dims):
    return lax.dot_general(a, b, dims, preferred_element_type=jnp.float32)


def live_count(segment_ref, image):
    first, last = STARTS[image] // 128, (STARTS[image] + SIZES[image]) // 128
    live = (segment_ref[first:last, :] >= 0).astype(jnp.float32)
    return jnp.sum(live).astype(jnp.int32)


def rows_of(image):
    return pl.ds(STARTS[image], SIZES[image])


def cols_of(head):
    return pl.ds(head * HS, HS)


def probs_kernel(
    segment_hbm, grad_hbm, q_hbm, k_hbm, v_hbm, proj_hbm,
    send_ref, segment_ref, q_ref, k_ref, v_ref, proj_ref, prob0_ref, prob1_ref, prob2_ref, total_ref,
    grad_ref, mean_ref, sems,
):
    prob_refs = (prob0_ref, prob1_ref, prob2_ref)
    copies = {}
    segment_copy = pltpu.make_async_copy(segment_hbm, segment_ref, sems.at[10])
    segment_copy.start()
    for image in range(IMG_DEV):
        rows = rows_of(image)
        for at, (src, dst) in enumerate(((q_hbm, q_ref), (k_hbm, k_ref), (v_hbm, v_ref))):
            copies[image, at] = pltpu.make_async_copy(src.at[rows], dst.at[rows], sems.at[image * 3 + at])
            copies[image, at].start()
    proj_copy = pltpu.make_async_copy(proj_hbm, proj_ref, sems.at[9])
    proj_copy.start()
    grad_copy = pltpu.make_async_copy(grad_hbm, grad_ref, sems.at[11])
    grad_copy.start()
    segment_copy.wait()
    mean_ref[...] = jnp.zeros_like(mean_ref)
    for image in range(IMG_DEV):
        size, rows = SIZES[image], rows_of(image)
        live = live_count(segment_ref, image)
        divisor = jnp.maximum(live, 1).astype(jnp.float32)
        ones = jnp.ones((size, HS), jnp.bfloat16)
        live_t = lax.broadcasted_iota(jnp.int32, (1, size), 1) < live
        for at in range(3):
            copies[image, at].wait()
        for head in range(HEADS_DEV):
            cols = cols_of(head)
            scores = dot(k_ref[rows, cols], q_ref[rows, cols], NT)
            if image != 1:
                live_u = lax.broadcasted_iota(jnp.int32, (size, size), 0) < live
                scores = jnp.where(live_u, scores, -1e30)
            weights = jnp.exp2((scores - jnp.max(scores, axis=0, keepdims=True)) * (SCALE * LOG2E))
            factor = jnp.where(live_t, 1.0 / jnp.sum(weights, axis=0, keepdims=True), 0.0)
            prob = weights * factor
            prob_refs[image][head] = prob
            total = dot(prob.astype(jnp.bfloat16), ones, NN)
            total_ref[rows, cols] = total
            summed = jnp.sum(total * v_ref[rows, cols].astype(jnp.float32), axis=0, keepdims=True)
            mean_ref[pl.ds(image, 1), cols] = summed / divisor
    proj_copy.wait()
    grad_copy.wait()
    grad = grad_ref[...].astype(jnp.float32)
    held = jnp.concatenate([jnp.zeros((3, WIDTH), jnp.float32), grad, jnp.zeros((2, WIDTH), jnp.float32)], axis=0)
    mean = mean_ref[...].astype(jnp.bfloat16)
    for peer in range(PEERS):
        share = dot(mean, proj_ref[:, pl.ds(peer * WIDTH, WIDTH)], NN)
        send_ref[peer] = (share + held).astype(jnp.bfloat16)


def grads_kernel(
    got_ref, segment_ref, q_ref, k_ref, v_ref, proj_ref, prob0_ref, prob1_ref, prob2_ref, total_ref,
    pooled_ref, dq_hbm, dk_hbm, dv_hbm,
    dq_ref, dk_ref, dv_ref, sems,
):
    prob_refs = (prob0_ref, prob1_ref, prob2_ref)
    summed = jnp.zeros((ROWS, WIDTH), jnp.float32)
    pooled = jnp.zeros((ROWS, WIDTH), jnp.float32)
    for peer in range(PEERS):
        got = got_ref[peer]
        pooled += got.astype(jnp.float32)
        summed += dot(got, proj_ref[:, pl.ds(peer * WIDTH, WIDTH)], NT)
    pooled_ref[...] = pooled[:IMG_DEV].astype(jnp.bfloat16)
    copies = []
    for image in (1, 2, 0):
        size, rows = SIZES[image], rows_of(image)
        divisor = jnp.maximum(live_count(segment_ref, image), 1).astype(jnp.float32)
        for head in range(HEADS_DEV):
            cols = cols_of(head)
            grad = (summed[3 + image : 4 + image, head * HS : (head + 1) * HS] / divisor).astype(jnp.bfloat16)
            grad_f = grad.astype(jnp.float32)
            across = dot(v_ref[rows, cols], jnp.broadcast_to(grad, (HS, HS)), NT) * SCALE
            across = jnp.concatenate([across] * (size // HS), axis=1)
            prob = prob_refs[image][head]
            delta = jnp.sum(prob * across, axis=0, keepdims=True)
            score_grad = (prob * (across - delta)).astype(jnp.bfloat16)
            dk_ref[rows, cols] = dot(score_grad, q_ref[rows, cols], NN).astype(jnp.bfloat16)
            dq_ref[rows, cols] = dot(score_grad, k_ref[rows, cols], TN).astype(jnp.bfloat16)
            dv_ref[rows, cols] = (total_ref[rows, cols] * grad_f).astype(jnp.bfloat16)
        for at, (src, dst) in enumerate(((dq_ref, dq_hbm), (dk_ref, dk_hbm), (dv_ref, dv_hbm))):
            copy = pltpu.make_async_copy(src.at[rows], dst.at[rows], sems.at[image * 3 + at])
            copy.start()
            copies.append(copy)
    for copy in copies:
        copy.wait()


def in_hbm(x):
    return pltpu.with_memory_space_constraint(x, pltpu.HBM)


def on_device(patch_queries, patch_keys, patch_values, out_proj, pool_grad, image_of_slot):
    segment = image_of_slot.reshape(SLOTS // 128, 128)
    here, anywhere = pl.BlockSpec(memory_space=pltpu.VMEM), pl.BlockSpec(memory_space=pl.ANY)
    patch = (SLOTS, WIDTH)
    bf16, f32 = jnp.bfloat16, jnp.float32
    kept_shapes = (
        ((SLOTS // 128, 128), jnp.int32), (patch, bf16), (patch, bf16), (patch, bf16), ((WIDTH, D), bf16),
        *(((HEADS_DEV, size, size), f32) for size in SIZES), (patch, f32),
    )
    send, *kept = pl.pallas_call(
        probs_kernel,
        out_shape=[pltpu.VMEM((PEERS, ROWS, WIDTH), bf16)] + [pltpu.VMEM(*s) for s in kept_shapes],
        in_specs=[anywhere] * 6,
        out_specs=[here] * 10,
        scratch_shapes=[
            pltpu.VMEM((IMG_DEV, WIDTH), bf16), pltpu.VMEM((ROWS, WIDTH), f32), pltpu.SemaphoreType.DMA((12,)),
        ],
        compiler_params=pltpu.CompilerParams(vmem_limit_bytes=VMEM_LIMIT),
        name="probs",
    )(*(in_hbm(x) for x in (segment, pool_grad, patch_queries, patch_keys, patch_values, out_proj)))
    got = lax.all_to_all(send, "heads", 0, 0, tiled=False)
    grad_shape = jax.ShapeDtypeStruct(patch, bf16)
    return pl.pallas_call(
        grads_kernel,
        out_shape=[jax.ShapeDtypeStruct((IMG_DEV, WIDTH), bf16)] + [grad_shape] * 3,
        in_specs=[here] * 10,
        out_specs=[here] + [anywhere] * 3,
        scratch_shapes=[pltpu.VMEM(patch, bf16)] * 3 + [pltpu.SemaphoreType.DMA((9,))],
        compiler_params=pltpu.CompilerParams(vmem_limit_bytes=VMEM_LIMIT),
        name="grads",
    )(got, *kept)


def solution(mesh):
    in_specs = (
        P("dp", "heads"),
        P("dp", "heads"),
        P("dp", "heads"),
        P("heads", None),
        P("dp", "heads"),
        P("dp"),
    )
    out_specs = (P("dp", "heads"), P("dp", "heads"), P("dp", "heads"), P("dp", "heads"))
    return jax.shard_map(
        on_device, mesh=mesh, in_specs=in_specs, out_specs=out_specs, check_vma=False
    )
```

time: 206 us -> 34.7 us (0.17)
  waiting for transfers between devices: 78.6 us -> 0 us
  matrix products: 43.6 us -> 0 us
  local copies, waits for them, and re-layouts: 20.3 us -> 0 us
  between operations: 15.6 us -> 0.64 us
  Pallas kernels: 0 us -> 12.5 us
  starting transfers between devices: 11.6 us -> 0 us
  other arithmetic: 9.74 us -> 0 us
  blocking collectives: 24.5 us -> 21.4 us
    unnamed x2 -> x0, waiting for transfers between devices: 69.1 us -> none
    dot_general x13 -> x0, matrix products: 33.8 us -> none  [the longest x2 6.95 us: backward_compute(): jnp.einsum('hqk,qhd->khd', score_grad, query_heads, preferred_element_typ...]
    all_gather x1 -> x0, blocking collectives: 24.5 us -> none  [token_grads(): lax.all_gather(grad_rows, 'heads', axis=1, tiled=True)]
    all_to_all x0 -> x1, blocking collectives: none -> 21.4 us  [on_device(): got = lax.all_to_all(send, 'heads', 0, 0, tiled=False)]
    pallas_call x0 -> x2, Pallas kernels: none -> 12.5 us  [the longest x1 6.67 us: on_device(): pl.pallas_call(grads_kernel, out_shape=[jax.ShapeDtypeStruct((IMG_DEV, WI...]
    ppermute x5 -> x0, starting transfers between devices: 11.6 us -> none  [passed_along(): return lax.ppermute(x, axis, pairs)]
    sub x4 -> x0, matrix products: 9.76 us -> none  [score_probs(): scores = scores - jnp.max(scores, axis=-1, keepdims=True)]
    ppermute x5 -> x0, waiting for transfers between devices: 9.49 us -> none  [passed_along(): return lax.ppermute(x, axis, pairs)]
  transfers between devices with their start and end apart: 6 -> 0, of which waited for: 3 -> 0; matrix products, arithmetic and copies ran while one was open for 22% -> 0% of each run, Pallas kernels for 0% -> 0%
where the time goes in v1:
time: 34.7 us; the launch traced here: 34.6 us
  blocking collectives  21.4 us (62%)
  Pallas kernels  12.5 us (36%)
  between operations  0.64 us (2%)
    all_to_all x1, blocking collectives, on_device(): got = lax.all_to_all(send, 'heads', 0, 0, tiled=False)  21.4 us
    pallas_call x1, Pallas kernels, on_device(): pl.pallas_call(grads_kernel, out_shape=[jax.ShapeDtypeStruct((IMG_DEV, WI...  6.67 us
    pallas_call x1, Pallas kernels, on_device(): pl.pallas_call(probs_kernel, out_shape=[pltpu.VMEM((PEERS, ROWS, WIDTH),...  5.81 us

profile of v1, /device:TPU:1, one launch (start us, length us, event | category | flops | bytes accessed | tf_op | source)
XLA Modules:
  0.0 34.6 jit_solution(3998880122381656250)
XLA Ops:
  0.6 5.8 %probs.1 = (bf16[16,8,384]{2,1,0:T(8,128)(2,1)S(1)}, s32[8,128]{1,0:T(8,128)S(1)}, bf16[1024,384]{1,0:T(8,128)(2,1)S(1)}, bf16[1024,384]{1,0:T(8,128)(2,1)S(1)},...) custom-call(s32[8,128]{1,0:T(8,128)} %bitcast.1, ...), custom_call_target="tpu_custom_call" | custom-call | tf_op jit(solution)/shard_map/probs/pallas_call | solution.py:149
  6.5 21.4 %all_to_all.5.got_ref = bf16[16,8,384]{2,1,0:T(8,128)(2,1)S(1)} all-to-all(bf16[16,8,384]{2,1,0:T(8,128)(2,1)S(1)} %get-tuple-element.14), channel_id=1, replica_groups=mesh['dp'=48,'heads'=16] {'heads'}, dimensions={0} | all-to-all | bytes 196608 | tf_op jit(solution)/shard_map/all_to_all | solution.py:160
  27.9 6.7 %grads.1 = (bf16[3,384]{1,0:T(4,128)(2,1)}, bf16[1024,384]{1,0:T(8,128)(2,1)}, bf16[1024,384]{1,0:T(8,128)(2,1)}, bf16[1024,384]{1,0:T(8,128)(2,1)}) custom-call(bf16[16,8,384]{2,1,0:T(8,128)(2,1)S(1)} %all_to_all.5.got_ref, s32[8,128]{1,0:T(8,128)S(1)} %get-tuple-element.15.segment_ref, bf16[1024,384]{1,0:T(8,128)(2,1)S(1)} %get-tuple-element.16.q_ref, ...), custom_call_target="tpu_custom_call" | custom-call | tf_op jit(solution)/shard_map/grads/pallas_call | solution.py:162

commit v2 on v1

v2 whole, which is shorter than its diff:
```python
import functools

import jax
import jax.numpy as jnp
from jax import lax
from jax.experimental import pallas as pl
from jax.experimental.pallas import tpu as pltpu
from jax.sharding import PartitionSpec as P

HS = 128
D = 6144
HEADS_DEV = 3
WIDTH = HEADS_DEV * HS
PEERS = 16
SLOTS = 1024
IMG_DEV = 3
STARTS = (0, 256, 640)
SIZES = (256, 384, 384)
SCALE = HS**-0.5
LOG2E = 1.4426950408889634
ROWS = 8
STRIP_A = 128
STRIP_B = 0
ORDER = (1, 2, 0)
VMEM_LIMIT = 24 * 2**20

NT = (((1,), (1,)), ((), ()))
NN = (((1,), (0,)), ((), ()))
TN = (((0,), (0,)), ((), ()))


def dot(a, b, dims):
    return lax.dot_general(a, b, dims, preferred_element_type=jnp.float32)


def live_count(segment_ref, image):
    first, last = STARTS[image] // 128, (STARTS[image] + SIZES[image]) // 128
    live = (segment_ref[first:last, :] >= 0).astype(jnp.float32)
    return jnp.sum(live).astype(jnp.int32)


def rows_of(image):
    return pl.ds(STARTS[image], SIZES[image])


def cols_of(head):
    return pl.ds(head * HS, HS)


def probs_kernel(
    segment_hbm, grad_hbm, q_hbm, k_hbm, v_hbm, proj_hbm,
    send_ref, segment_ref, q_ref, k_ref, v_ref, proj_ref, prob0_ref, prob1_ref, prob2_ref, total_ref,
    grad_ref, share_ref, score_ref, sems,
):
    prob_refs = (prob0_ref, prob1_ref, prob2_ref)
    copies = {}

    def fetch(key, src, dst):
        copies[key] = pltpu.make_async_copy(src, dst, sems.at[len(copies)])
        copies[key].start()

    def arrive(*keys):
        for key in keys:
            copies[key].wait()

    fetch("segment", segment_hbm, segment_ref)
    for image in range(IMG_DEV):
        rows = rows_of(image)
        for name, src, dst in (("q", q_hbm, q_ref), ("k", k_hbm, k_ref), ("v", v_hbm, v_ref)):
            fetch((name, image), src.at[rows], dst.at[rows])
    fetch("grad", grad_hbm, grad_ref)
    for head in range(HEADS_DEV):
        rows = cols_of(head)
        fetch(("proj", head), proj_hbm.at[rows], proj_ref.at[rows])
    arrive("segment")
    live = [live_count(segment_ref, image) for image in range(IMG_DEV)]

    def score(image, head):
        rows, cols = rows_of(image), cols_of(head)
        scores = dot(k_ref[rows, cols], q_ref[rows, cols], NT)
        slots[image, head] = len(slots) % 3
        score_ref[slots[image, head], pl.ds(0, SIZES[image]), pl.ds(0, SIZES[image])] = scores

    def unit(image, head):
        size, rows, cols = SIZES[image], rows_of(image), cols_of(head)
        width = STRIP_A or size
        for first in range(0, size, width):
            scores = score_ref[slots[image, head], pl.ds(0, size), pl.ds(first, width)]
            if image != 1:
                live_u = lax.broadcasted_iota(jnp.int32, (size, width), 0) < live[image]
                scores = jnp.where(live_u, scores, -1e30)
            weights = jnp.exp2((scores - jnp.max(scores, axis=0, keepdims=True)) * (SCALE * LOG2E))
            live_t = lax.broadcasted_iota(jnp.int32, (1, width), 1) + first < live[image]
            factor = jnp.where(live_t, 1.0 / jnp.sum(weights, axis=0, keepdims=True), 0.0)
            prob_refs[image][head, :, pl.ds(first, width)] = weights * factor
        total = jnp.sum(prob_refs[image][head], axis=1, keepdims=True)
        total_ref[rows, cols] = jnp.broadcast_to(total, (size, HS))
        summed = jnp.sum(total * v_ref[rows, cols].astype(jnp.float32), axis=0, keepdims=True)
        means[image, head] = summed / jnp.maximum(live[image], 1).astype(jnp.float32)

    def project(head):
        mean = jnp.concatenate([means[image, head] for image in range(IMG_DEV)] + [jnp.zeros((5, HS), jnp.float32)], axis=0)
        return dot(mean.astype(jnp.bfloat16), proj_ref[cols_of(head), :], NN)

    means, slots = {}, {}
    arrive(*((name, 0) for name in "qkv"))
    score(0, 0)
    score(0, 1)
    unit(0, 0)
    score(0, 2)
    unit(0, 1)
    arrive(*((name, image) for image in (1, 2) for name in "qkv"))
    score(1, 0)
    unit(0, 2)
    score(2, 0)
    unit(1, 0)
    score(1, 1)
    unit(2, 0)
    score(2, 1)
    arrive(("proj", 0))
    share_ref[...] = project(0)
    unit(1, 1)
    score(1, 2)
    unit(2, 1)
    score(2, 2)
    arrive(("proj", 1), ("proj", 2))
    share_ref[...] += project(1)
    unit(1, 2)
    unit(2, 2)
    share = share_ref[...] + project(2)
    arrive("grad")
    grad = grad_ref[...].astype(jnp.float32)
    held = jnp.concatenate([jnp.zeros((3, WIDTH), jnp.float32), grad, jnp.zeros((2, WIDTH), jnp.float32)], axis=0)
    for peer in range(PEERS):
        send_ref[peer] = (share[:, peer * WIDTH : (peer + 1) * WIDTH] + held).astype(jnp.bfloat16)


def grads_kernel(
    got_ref, segment_ref, q_ref, k_ref, v_ref, proj_ref, prob0_ref, prob1_ref, prob2_ref, total_ref,
    pooled_ref, dq_hbm, dk_hbm, dv_hbm,
    dq_ref, dk_ref, dv_ref, score_ref, sems,
):
    prob_refs = (prob0_ref, prob1_ref, prob2_ref)
    copies = []

    def send(image, *pairs):
        rows = rows_of(image)
        for src, dst in pairs:
            copy = pltpu.make_async_copy(src.at[rows], dst.at[rows], sems.at[len(copies)])
            copy.start()
            copies.append(copy)

    got = [got_ref[peer] for peer in range(PEERS)]
    gathered = jnp.concatenate(got, axis=1)
    divisor = [
        jnp.maximum(live_count(segment_ref, image), 1).astype(jnp.float32) for image in range(IMG_DEV)
    ]

    def project(head):
        return dot(gathered, proj_ref[cols_of(head), :], NT)

    def score(image, head):
        size, rows, cols = SIZES[image], rows_of(image), cols_of(head)
        width = STRIP_B or size
        grad = (summed[head][3 + image : 4 + image] / divisor[image]).astype(jnp.bfloat16).astype(jnp.float32)
        across = jnp.sum(v_ref[rows, cols].astype(jnp.float32) * (grad * SCALE), axis=1, keepdims=True)
        dv_ref[rows, cols] = (total_ref[rows, cols] * grad).astype(jnp.bfloat16)
        for first in range(0, size, width):
            prob = prob_refs[image][head, :, pl.ds(first, width)]
            delta = jnp.sum(prob * across, axis=0, keepdims=True)
            score_ref[head, pl.ds(0, size), pl.ds(first, width)] = (prob * (across - delta)).astype(jnp.bfloat16)

    def unit(image, head):
        size, rows, cols = SIZES[image], rows_of(image), cols_of(head)
        score_grad = score_ref[head, pl.ds(0, size), pl.ds(0, size)]
        dk_ref[rows, cols] = dot(score_grad, q_ref[rows, cols], NN).astype(jnp.bfloat16)
        dq_ref[rows, cols] = dot(score_grad, k_ref[rows, cols], TN).astype(jnp.bfloat16)

    summed = [project(0)]
    units = [(image, head) for image in ORDER for head in range(HEADS_DEV)]
    for at, (image, head) in enumerate(units):
        if at + 1 < HEADS_DEV:
            summed.append(project(at + 1))
        score(image, head)
        if at > 0:
            unit(*units[at - 1])
        if head == 0 and at > 0:
            send(units[at - 1][0], (dq_ref, dq_hbm), (dk_ref, dk_hbm), (dv_ref, dv_hbm))
        if at == HEADS_DEV:
            pooled = got[0].astype(jnp.float32)
            for piece in got[1:]:
                pooled += piece.astype(jnp.float32)
            pooled_ref[...] = pooled[:IMG_DEV].astype(jnp.bfloat16)
    unit(*units[-1])
    send(ORDER[2], (dq_ref, dq_hbm), (dk_ref, dk_hbm), (dv_ref, dv_hbm))
    for copy in copies:
        copy.wait()


def in_hbm(x):
    return pltpu.with_memory_space_constraint(x, pltpu.HBM)


def on_device(patch_queries, patch_keys, patch_values, out_proj, pool_grad, image_of_slot):
    segment = image_of_slot.reshape(SLOTS // 128, 128)
    here, anywhere = pl.BlockSpec(memory_space=pltpu.VMEM), pl.BlockSpec(memory_space=pl.ANY)
    patch = (SLOTS, WIDTH)
    bf16, f32 = jnp.bfloat16, jnp.float32
    kept_shapes = (
        ((SLOTS // 128, 128), jnp.int32), (patch, bf16), (patch, bf16), (patch, bf16), ((WIDTH, D), bf16),
        *(((HEADS_DEV, size, size), f32) for size in SIZES), (patch, f32),
    )
    send, *kept = pl.pallas_call(
        probs_kernel,
        out_shape=[pltpu.VMEM((PEERS, ROWS, WIDTH), bf16)] + [pltpu.VMEM(*s) for s in kept_shapes],
        in_specs=[anywhere] * 6,
        out_specs=[here] * 10,
        scratch_shapes=[
            pltpu.VMEM((IMG_DEV, WIDTH), bf16), pltpu.VMEM((ROWS, D), f32),
            pltpu.VMEM((3, max(SIZES), max(SIZES)), f32), pltpu.SemaphoreType.DMA((14,)),
        ],
        compiler_params=pltpu.CompilerParams(vmem_limit_bytes=VMEM_LIMIT),
        name="probs",
    )(*(in_hbm(x) for x in (segment, pool_grad, patch_queries, patch_keys, patch_values, out_proj)))
    got = lax.all_to_all(send, "heads", 0, 0, tiled=False)
    grad_shape = jax.ShapeDtypeStruct(patch, bf16)
    return pl.pallas_call(
        grads_kernel,
        out_shape=[jax.ShapeDtypeStruct((IMG_DEV, WIDTH), bf16)] + [grad_shape] * 3,
        in_specs=[here] * 10,
        out_specs=[here] + [anywhere] * 3,
        scratch_shapes=[pltpu.VMEM(patch, bf16)] * 3
        + [pltpu.VMEM((IMG_DEV, max(SIZES), max(SIZES)), bf16), pltpu.SemaphoreType.DMA((9,))],
        compiler_params=pltpu.CompilerParams(vmem_limit_bytes=VMEM_LIMIT),
        name="grads",
    )(got, *kept)


def solution(mesh):
    in_specs = (
        P("dp", "heads"),
        P("dp", "heads"),
        P("dp", "heads"),
        P("heads", None),
        P("dp", "heads"),
        P("dp"),
    )
    out_specs = (P("dp", "heads"), P("dp", "heads"), P("dp", "heads"), P("dp", "heads"))
    return jax.shard_map(
        on_device, mesh=mesh, in_specs=in_specs, out_specs=out_specs, check_vma=False
    )
```

time: 34.7 us -> 31.9 us (0.919)
  Pallas kernels: 12.5 us -> 9.74 us
    pallas_call x1, Pallas kernels: 5.81 us -> 4.37 us  [on_device(): pl.pallas_call(probs_kernel, out_shape=[pltpu.VMEM((PEERS, ROWS, WIDTH),...]
    pallas_call x1, Pallas kernels: 6.67 us -> 5.36 us  [on_device(): pl.pallas_call(grads_kernel, out_shape=[jax.ShapeDtypeStruct((IMG_DEV, WI...]
where the time goes in v2:
time: 31.9 us; the launch traced here: 31.8 us
  blocking collectives  21.4 us (67%)
  Pallas kernels  9.74 us (31%)
  between operations  0.64 us (2%)
    all_to_all x1, blocking collectives, on_device(): got = lax.all_to_all(send, 'heads', 0, 0, tiled=False)  21.4 us
    pallas_call x1, Pallas kernels, on_device(): pl.pallas_call(grads_kernel, out_shape=[jax.ShapeDtypeStruct((IMG_DEV, WI...  5.36 us
    pallas_call x1, Pallas kernels, on_device(): pl.pallas_call(probs_kernel, out_shape=[pltpu.VMEM((PEERS, ROWS, WIDTH),...  4.37 us

profile of v2, /device:TPU:1, one launch (start us, length us, event | category | flops | bytes accessed | tf_op | source)
XLA Modules:
  0.0 31.8 jit_solution(11833658766845207126)
XLA Ops:
  0.6 4.4 %probs.1 = (bf16[16,8,384]{2,1,0:T(8,128)(2,1)S(1)}, s32[8,128]{1,0:T(8,128)S(1)}, bf16[1024,384]{1,0:T(8,128)(2,1)S(1)}, bf16[1024,384]{1,0:T(8,128)(2,1)S(1)},...) custom-call(s32[8,128]{1,0:T(8,128)} %bitcast.1, ...), custom_call_target="tpu_custom_call" | custom-call | tf_op jit(solution)/shard_map/probs/pallas_call | solution.py:213
  5.0 21.4 %all_to_all.5.got_ref = bf16[16,8,384]{2,1,0:T(8,128)(2,1)S(1)} all-to-all(bf16[16,8,384]{2,1,0:T(8,128)(2,1)S(1)} %get-tuple-element.14), channel_id=1, replica_groups=mesh['dp'=48,'heads'=16] {'heads'}, dimensions={0} | all-to-all | bytes 196608 | tf_op jit(solution)/shard_map/all_to_all | solution.py:225
  26.4 5.4 %grads.1 = (bf16[3,384]{1,0:T(4,128)(2,1)}, bf16[1024,384]{1,0:T(8,128)(2,1)}, bf16[1024,384]{1,0:T(8,128)(2,1)}, bf16[1024,384]{1,0:T(8,128)(2,1)}) custom-call(bf16[16,8,384]{2,1,0:T(8,128)(2,1)S(1)} %all_to_all.5.got_ref, s32[8,128]{1,0:T(8,128)S(1)} %get-tuple-element.15.segment_ref, bf16[1024,384]{1,0:T(8,128)(2,1)S(1)} %get-tuple-element.16.q_ref, ...), custom_call_target="tpu_custom_call" | custom-call | tf_op jit(solution)/shard_map/grads/pallas_call | solution.py:227

commit v3 on v2

--- a/solution.py
+++ b/solution.py
@@ -75,9 +75,21 @@
     arrive("segment")
     live = [live_count(segment_ref, image) for image in range(IMG_DEV)]
 
+    first_lane = lax.broadcasted_iota(jnp.int32, (max(SIZES), HS), 1) == 0
+    slot = lax.broadcasted_iota(jnp.int32, (max(SIZES), HS), 0)
+    ones = jnp.where(first_lane, 1.0, 0.0).astype(jnp.bfloat16)
+    dead = {
+        image: jnp.where(first_lane & (slot >= live[image]), -1e30, 0.0).astype(jnp.bfloat16)[: SIZES[image]]
+        for image in (0, 2)
+    }
+
     def score(image, head):
         rows, cols = rows_of(image), cols_of(head)
-        scores = dot(k_ref[rows, cols], q_ref[rows, cols], NT)
+        keys, queries = k_ref[rows, cols], q_ref[rows, cols]
+        if image != 1:
+            keys = jnp.concatenate([keys, dead[image]], axis=1)
+            queries = jnp.concatenate([queries, ones[: SIZES[image]]], axis=1)
+        scores = dot(keys, queries, NT)
         slots[image, head] = len(slots) % 3
         score_ref[slots[image, head], pl.ds(0, SIZES[image]), pl.ds(0, SIZES[image])] = scores
 
@@ -86,9 +98,6 @@
         width = STRIP_A or size
         for first in range(0, size, width):
             scores = score_ref[slots[image, head], pl.ds(0, size), pl.ds(first, width)]
-            if image != 1:
-                live_u = lax.broadcasted_iota(jnp.int32, (size, width), 0) < live[image]
-                scores = jnp.where(live_u, scores, -1e30)
             weights = jnp.exp2((scores - jnp.max(scores, axis=0, keepdims=True)) * (SCALE * LOG2E))
             live_t = lax.broadcasted_iota(jnp.int32, (1, width), 1) + first < live[image]
             factor = jnp.where(live_t, 1.0 / jnp.sum(weights, axis=0, keepdims=True), 0.0)
@@ -123,22 +132,25 @@
     score(1, 2)
     unit(2, 1)
     score(2, 2)
-    arrive(("proj", 1), ("proj", 2))
+    arrive(("proj", 1))
     share_ref[...] += project(1)
     unit(1, 2)
     unit(2, 2)
-    share = share_ref[...] + project(2)
+    arrive(("proj", 2))
+    share_ref[...] += project(2)
     arrive("grad")
     grad = grad_ref[...].astype(jnp.float32)
-    held = jnp.concatenate([jnp.zeros((3, WIDTH), jnp.float32), grad, jnp.zeros((2, WIDTH), jnp.float32)], axis=0)
+    grad = jnp.concatenate([grad[image : image + 1] for image in range(IMG_DEV)], axis=1)
     for peer in range(PEERS):
-        send_ref[peer] = (share[:, peer * WIDTH : (peer + 1) * WIDTH] + held).astype(jnp.bfloat16)
+        share = [share_ref[pl.ds(image, 1), pl.ds(peer * WIDTH, WIDTH)] for image in range(IMG_DEV)]
+        message = jnp.concatenate([jnp.concatenate(share, axis=1), grad], axis=0)
+        send_ref[peer] = message.astype(jnp.bfloat16)
 
 
 def grads_kernel(
     got_ref, segment_ref, q_ref, k_ref, v_ref, proj_ref, prob0_ref, prob1_ref, prob2_ref, total_ref,
     pooled_ref, dq_hbm, dk_hbm, dv_hbm,
-    dq_ref, dk_ref, dv_ref, score_ref, sems,
+    dq_ref, dk_ref, dv_ref, score_ref, gathered_ref, sems,
 ):
     prob_refs = (prob0_ref, prob1_ref, prob2_ref)
     copies = []
@@ -150,8 +162,12 @@
             copy.start()
             copies.append(copy)
 
-    got = [got_ref[peer] for peer in range(PEERS)]
-    gathered = jnp.concatenate(got, axis=1)
+    got = [got_ref[peer].astype(jnp.float32) for peer in range(PEERS)]
+    for peer in range(PEERS):
+        for image in range(IMG_DEV):
+            piece = got[peer][1:, image * WIDTH : (image + 1) * WIDTH]
+            gathered_ref[pl.ds(image, 1), pl.ds(peer * WIDTH, WIDTH)] = piece
+    gathered = gathered_ref[pl.ds(0, IMG_DEV), :].astype(jnp.bfloat16)
     divisor = [
         jnp.maximum(live_count(segment_ref, image), 1).astype(jnp.float32) for image in range(IMG_DEV)
     ]
@@ -162,7 +178,7 @@
     def score(image, head):
         size, rows, cols = SIZES[image], rows_of(image), cols_of(head)
         width = STRIP_B or size
-        grad = (summed[head][3 + image : 4 + image] / divisor[image]).astype(jnp.bfloat16).astype(jnp.float32)
+        grad = (summed[head][image : image + 1] / divisor[image]).astype(jnp.bfloat16).astype(jnp.float32)
         across = jnp.sum(v_ref[rows, cols].astype(jnp.float32) * (grad * SCALE), axis=1, keepdims=True)
         dv_ref[rows, cols] = (total_ref[rows, cols] * grad).astype(jnp.bfloat16)
         for first in range(0, size, width):
@@ -179,18 +195,19 @@
     summed = [project(0)]
     units = [(image, head) for image in ORDER for head in range(HEADS_DEV)]
     for at, (image, head) in enumerate(units):
+        score(image, head)
         if at + 1 < HEADS_DEV:
             summed.append(project(at + 1))
-        score(image, head)
         if at > 0:
             unit(*units[at - 1])
         if head == 0 and at > 0:
             send(units[at - 1][0], (dq_ref, dq_hbm), (dk_ref, dk_hbm), (dv_ref, dv_hbm))
         if at == HEADS_DEV:
-            pooled = got[0].astype(jnp.float32)
+            pooled = got[0][:1]
             for piece in got[1:]:
-                pooled += piece.astype(jnp.float32)
-            pooled_ref[...] = pooled[:IMG_DEV].astype(jnp.bfloat16)
+                pooled += piece[:1]
+            pooled = jnp.concatenate([pooled[:, m * WIDTH : (m + 1) * WIDTH] for m in range(IMG_DEV)], axis=0)
+            pooled_ref[...] = pooled.astype(jnp.bfloat16)
     unit(*units[-1])
     send(ORDER[2], (dq_ref, dq_hbm), (dk_ref, dk_hbm), (dv_ref, dv_hbm))
     for copy in copies:
@@ -212,7 +229,7 @@
     )
     send, *kept = pl.pallas_call(
         probs_kernel,
-        out_shape=[pltpu.VMEM((PEERS, ROWS, WIDTH), bf16)] + [pltpu.VMEM(*s) for s in kept_shapes],
+        out_shape=[pltpu.VMEM((PEERS, 2, IMG_DEV * WIDTH), bf16)] + [pltpu.VMEM(*s) for s in kept_shapes],
         in_specs=[anywhere] * 6,
         out_specs=[here] * 10,
         scratch_shapes=[
@@ -230,7 +247,7 @@
         in_specs=[here] * 10,
         out_specs=[here] + [anywhere] * 3,
         scratch_shapes=[pltpu.VMEM(patch, bf16)] * 3
-        + [pltpu.VMEM((IMG_DEV, max(SIZES), max(SIZES)), bf16), pltpu.SemaphoreType.DMA((9,))],
+        + [pltpu.VMEM((IMG_DEV, max(SIZES), max(SIZES)), bf16), pltpu.VMEM((ROWS, D), f32), pltpu.SemaphoreType.DMA((9,))],
         compiler_params=pltpu.CompilerParams(vmem_limit_bytes=VMEM_LIMIT),
         name="grads",
     )(got, *kept)

time: 31.9 us -> 31.4 us (0.984)
  blocking collectives: 21.4 us -> 20.9 us
    all_to_all x1, blocking collectives: 21.4 us -> 20.9 us  [on_device(): got = lax.all_to_all(send, 'heads', 0, 0, tiled=False)]
where the time goes in v3:
time: 31.4 us; the launch traced here: 31.2 us
  blocking collectives  20.9 us (67%)
  Pallas kernels  9.67 us (31%)
  between operations  0.64 us (2%)
    all_to_all x1, blocking collectives, on_device(): got = lax.all_to_all(send, 'heads', 0, 0, tiled=False)  20.9 us
    pallas_call x1, Pallas kernels, on_device(): pl.pallas_call(grads_kernel, out_shape=[jax.ShapeDtypeStruct((IMG_DEV, WI...  5.36 us
    pallas_call x1, Pallas kernels, on_device(): pl.pallas_call(probs_kernel, out_shape=[pltpu.VMEM((PEERS, 2, IMG_DEV * W...  4.31 us

profile of v3, /device:TPU:1, one launch (start us, length us, event | category | flops | bytes accessed | tf_op | source)
XLA Modules:
  0.0 31.2 jit_solution(319147745975331091)
XLA Ops:
  0.6 4.3 %probs.1 = (bf16[16,2,1152]{2,1,0:T(2,128)(2,1)S(1)}, s32[8,128]{1,0:T(8,128)S(1)}, bf16[1024,384]{1,0:T(8,128)(2,1)S(1)}, bf16[1024,384]{1,0:T(8,128)(2,1)S(1)}...) custom-call(s32[8,128]{1,0:T(8,128)} %bitcast.1, ...), custom_call_target="tpu_custom_call" | custom-call | tf_op jit(solution)/shard_map/probs/pallas_call | solution.py:230
  4.9 20.9 %all_to_all.5.got_ref = bf16[16,2,1152]{2,1,0:T(2,128)(2,1)S(1)} all-to-all(bf16[16,2,1152]{2,1,0:T(2,128)(2,1)S(1)} %get-tuple-element.14), channel_id=1, replica_groups=mesh['dp'=48,'heads'=16] {'heads'}, dimensions={0} | all-to-all | bytes 147456 | tf_op jit(solution)/shard_map/all_to_all | solution.py:242
  25.9 5.4 %grads.1 = (bf16[3,384]{1,0:T(4,128)(2,1)}, bf16[1024,384]{1,0:T(8,128)(2,1)}, bf16[1024,384]{1,0:T(8,128)(2,1)}, bf16[1024,384]{1,0:T(8,128)(2,1)}) custom-call(bf16[16,2,1152]{2,1,0:T(2,128)(2,1)S(1)} %all_to_all.5.got_ref, s32[8,128]{1,0:T(8,128)S(1)} %get-tuple-element.15.segment_ref, bf16[1024,384]{1,0:T(8,128)(2,1)S(1)} %get-tuple-element.16.q_ref, ...), custom_call_target="tpu_custom_call" | custom-call | tf_op jit(solution)/shard_map/grads/pallas_call | solution.py:244

commit v4 on v3

--- a/solution.py
+++ b/solution.py
@@ -96,13 +96,16 @@
     def unit(image, head):
         size, rows, cols = SIZES[image], rows_of(image), cols_of(head)
         width = STRIP_A or size
+        total = jnp.zeros((size, HS), jnp.float32)
         for first in range(0, size, width):
             scores = score_ref[slots[image, head], pl.ds(0, size), pl.ds(first, width)]
             weights = jnp.exp2((scores - jnp.max(scores, axis=0, keepdims=True)) * (SCALE * LOG2E))
             live_t = lax.broadcasted_iota(jnp.int32, (1, width), 1) + first < live[image]
             factor = jnp.where(live_t, 1.0 / jnp.sum(weights, axis=0, keepdims=True), 0.0)
-            prob_refs[image][head, :, pl.ds(first, width)] = weights * factor
-        total = jnp.sum(prob_refs[image][head], axis=1, keepdims=True)
+            prob = weights * factor
+            prob_refs[image][head, :, pl.ds(first, width)] = prob
+            total += prob
+        total = jnp.sum(total, axis=1, keepdims=True)
         total_ref[rows, cols] = jnp.broadcast_to(total, (size, HS))
         summed = jnp.sum(total * v_ref[rows, cols].astype(jnp.float32), axis=0, keepdims=True)
         means[image, head] = summed / jnp.maximum(live[image], 1).astype(jnp.float32)
@@ -112,9 +115,10 @@
         return dot(mean.astype(jnp.bfloat16), proj_ref[cols_of(head), :], NN)
 
     means, slots = {}, {}
-    arrive(*((name, 0) for name in "qkv"))
+    arrive(("q", 0), ("k", 0))
     score(0, 0)
     score(0, 1)
+    arrive(("v", 0))
     unit(0, 0)
     score(0, 2)
     unit(0, 1)
@@ -149,8 +153,8 @@
 
 def grads_kernel(
     got_ref, segment_ref, q_ref, k_ref, v_ref, proj_ref, prob0_ref, prob1_ref, prob2_ref, total_ref,
-    pooled_ref, dq_hbm, dk_hbm, dv_hbm,
-    dq_ref, dk_ref, dv_ref, score_ref, gathered_ref, sems,
+    pooled_hbm, dq_hbm, dk_hbm, dv_hbm,
+    pooled_ref, dq_ref, dk_ref, dv_ref, score_ref, gathered_ref, sems,
 ):
     prob_refs = (prob0_ref, prob1_ref, prob2_ref)
     copies = []
@@ -162,6 +166,7 @@
             copy.start()
             copies.append(copy)
 
+    pooled_copy = pltpu.make_async_copy(pooled_ref, pooled_hbm, sems.at[9])
     got = [got_ref[peer].astype(jnp.float32) for peer in range(PEERS)]
     for peer in range(PEERS):
         for image in range(IMG_DEV):
@@ -202,14 +207,17 @@
             unit(*units[at - 1])
         if head == 0 and at > 0:
             send(units[at - 1][0], (dq_ref, dq_hbm), (dk_ref, dk_hbm), (dv_ref, dv_hbm))
-        if at == HEADS_DEV:
+        if at == 0:
             pooled = got[0][:1]
             for piece in got[1:]:
                 pooled += piece[:1]
             pooled = jnp.concatenate([pooled[:, m * WIDTH : (m + 1) * WIDTH] for m in range(IMG_DEV)], axis=0)
             pooled_ref[...] = pooled.astype(jnp.bfloat16)
+            pooled_copy.start()
+    send(ORDER[2], (dv_ref, dv_hbm))
     unit(*units[-1])
-    send(ORDER[2], (dq_ref, dq_hbm), (dk_ref, dk_hbm), (dv_ref, dv_hbm))
+    send(ORDER[2], (dq_ref, dq_hbm), (dk_ref, dk_hbm))
+    pooled_copy.wait()
     for copy in copies:
         copy.wait()
 
@@ -245,9 +253,9 @@
         grads_kernel,
         out_shape=[jax.ShapeDtypeStruct((IMG_DEV, WIDTH), bf16)] + [grad_shape] * 3,
         in_specs=[here] * 10,
-        out_specs=[here] + [anywhere] * 3,
-        scratch_shapes=[pltpu.VMEM(patch, bf16)] * 3
-        + [pltpu.VMEM((IMG_DEV, max(SIZES), max(SIZES)), bf16), pltpu.VMEM((ROWS, D), f32), pltpu.SemaphoreType.DMA((9,))],
+        out_specs=[anywhere] * 4,
+        scratch_shapes=[pltpu.VMEM((IMG_DEV, WIDTH), bf16)] + [pltpu.VMEM(patch, bf16)] * 3
+        + [pltpu.VMEM((IMG_DEV, max(SIZES), max(SIZES)), bf16), pltpu.VMEM((ROWS, D), f32), pltpu.SemaphoreType.DMA((10,))],
         compiler_params=pltpu.CompilerParams(vmem_limit_bytes=VMEM_LIMIT),
         name="grads",
     )(got, *kept)

time: 31.4 us -> 30.8 us (0.981)
  Pallas kernels: 9.67 us -> 9.04 us
    pallas_call x1, Pallas kernels: 5.36 us -> 4.74 us  [on_device(): pl.pallas_call(grads_kernel, out_shape=[jax.ShapeDtypeStruct((IMG_DEV, WI...]
where the time goes in v4:
time: 30.8 us; the launch traced here: 30.6 us
  blocking collectives  20.9 us (68%)
  Pallas kernels  9.04 us (29%)
  between operations  0.64 us (2%)
    all_to_all x1, blocking collectives, on_device(): got = lax.all_to_all(send, 'heads', 0, 0, tiled=False)  20.9 us
    pallas_call x1, Pallas kernels, on_device(): pl.pallas_call(grads_kernel, out_shape=[jax.ShapeDtypeStruct((IMG_DEV, WI...  4.74 us
    pallas_call x1, Pallas kernels, on_device(): pl.pallas_call(probs_kernel, out_shape=[pltpu.VMEM((PEERS, 2, IMG_DEV * W...  4.3 us

profile of v4, /device:TPU:1, one launch (start us, length us, event | category | flops | bytes accessed | tf_op | source)
XLA Modules:
  0.0 30.6 jit_solution(9082942386620517807)
XLA Ops:
  0.6 4.3 %probs.1 = (bf16[16,2,1152]{2,1,0:T(2,128)(2,1)S(1)}, s32[8,128]{1,0:T(8,128)S(1)}, bf16[1024,384]{1,0:T(8,128)(2,1)S(1)}, bf16[1024,384]{1,0:T(8,128)(2,1)S(1)}...) custom-call(s32[8,128]{1,0:T(8,128)} %bitcast.1, ...), custom_call_target="tpu_custom_call" | custom-call | tf_op jit(solution)/shard_map/probs/pallas_call | solution.py:238
  4.9 20.9 %all_to_all.5.got_ref = bf16[16,2,1152]{2,1,0:T(2,128)(2,1)S(1)} all-to-all(bf16[16,2,1152]{2,1,0:T(2,128)(2,1)S(1)} %get-tuple-element.14), channel_id=1, replica_groups=mesh['dp'=48,'heads'=16] {'heads'}, dimensions={0} | all-to-all | bytes 147456 | tf_op jit(solution)/shard_map/all_to_all | solution.py:250
  25.9 4.7 %grads.1 = (bf16[3,384]{1,0:T(4,128)(2,1)}, bf16[1024,384]{1,0:T(8,128)(2,1)}, bf16[1024,384]{1,0:T(8,128)(2,1)}, bf16[1024,384]{1,0:T(8,128)(2,1)}) custom-call(bf16[16,2,1152]{2,1,0:T(2,128)(2,1)S(1)} %all_to_all.5.got_ref, s32[8,128]{1,0:T(8,128)S(1)} %get-tuple-element.15.segment_ref, bf16[1024,384]{1,0:T(8,128)(2,1)S(1)} %get-tuple-element.16.q_ref, ...), custom_call_target="tpu_custom_call" | custom-call | tf_op jit(solution)/shard_map/grads/pallas_call | solution.py:252

commit v5 on v4

--- a/solution.py
+++ b/solution.py
@@ -47,9 +47,13 @@
     return pl.ds(head * HS, HS)
 
 
+def enters_last():
+    return (lax.axis_index("dp") == 0) & (lax.axis_index("heads") == 0)
+
+
 def probs_kernel(
     segment_hbm, grad_hbm, q_hbm, k_hbm, v_hbm, proj_hbm,
-    send_ref, segment_ref, q_ref, k_ref, v_ref, proj_ref, prob0_ref, prob1_ref, prob2_ref, total_ref,
+    send_ref, segment_ref, q_ref, k_ref, v_ref, proj_ref, turned_ref, prob0_ref, prob1_ref, prob2_ref, total_ref,
     grad_ref, share_ref, score_ref, sems,
 ):
     prob_refs = (prob0_ref, prob1_ref, prob2_ref)
@@ -150,11 +154,18 @@
         message = jnp.concatenate([jnp.concatenate(share, axis=1), grad], axis=0)
         send_ref[peer] = message.astype(jnp.bfloat16)
 
+    @pl.when(jnp.logical_not(enters_last()))
+    def _():
+        @pl.loop(0, PEERS)
+        def _(peer):
+            block = pl.ds(pl.multiple_of(peer * WIDTH, WIDTH), WIDTH)
+            turned_ref[block, :] = jnp.transpose(proj_ref[:, block])
+
 
 def grads_kernel(
-    got_ref, segment_ref, q_ref, k_ref, v_ref, proj_ref, prob0_ref, prob1_ref, prob2_ref, total_ref,
+    got_ref, segment_ref, q_ref, k_ref, v_ref, proj_ref, turned_ref, prob0_ref, prob1_ref, prob2_ref, total_ref,
     pooled_hbm, dq_hbm, dk_hbm, dv_hbm,
-    pooled_ref, dq_ref, dk_ref, dv_ref, score_ref, gathered_ref, sems,
+    pooled_ref, dq_ref, dk_ref, dv_ref, score_ref, gathered_ref, summed_ref, sems,
 ):
     prob_refs = (prob0_ref, prob1_ref, prob2_ref)
     copies = []
@@ -177,13 +188,18 @@
         jnp.maximum(live_count(segment_ref, image), 1).astype(jnp.float32) for image in range(IMG_DEV)
     ]
 
-    def project(head):
-        return dot(gathered, proj_ref[cols_of(head), :], NT)
+    @pl.when(enters_last())
+    def _():
+        summed_ref[...] = dot(gathered, proj_ref[...], NT)
+
+    @pl.when(jnp.logical_not(enters_last()))
+    def _():
+        summed_ref[...] = dot(gathered, turned_ref[...], NN)
 
     def score(image, head):
         size, rows, cols = SIZES[image], rows_of(image), cols_of(head)
         width = STRIP_B or size
-        grad = (summed[head][image : image + 1] / divisor[image]).astype(jnp.bfloat16).astype(jnp.float32)
+        grad = (summed_ref[pl.ds(image, 1), cols] / divisor[image]).astype(jnp.bfloat16).astype(jnp.float32)
         across = jnp.sum(v_ref[rows, cols].astype(jnp.float32) * (grad * SCALE), axis=1, keepdims=True)
         dv_ref[rows, cols] = (total_ref[rows, cols] * grad).astype(jnp.bfloat16)
         for first in range(0, size, width):
@@ -197,12 +213,9 @@
         dk_ref[rows, cols] = dot(score_grad, q_ref[rows, cols], NN).astype(jnp.bfloat16)
         dq_ref[rows, cols] = dot(score_grad, k_ref[rows, cols], TN).astype(jnp.bfloat16)
 
-    summed = [project(0)]
     units = [(image, head) for image in ORDER for head in range(HEADS_DEV)]
     for at, (image, head) in enumerate(units):
         score(image, head)
-        if at + 1 < HEADS_DEV:
-            summed.append(project(at + 1))
         if at > 0:
             unit(*units[at - 1])
         if head == 0 and at > 0:
@@ -232,14 +245,14 @@
     patch = (SLOTS, WIDTH)
     bf16, f32 = jnp.bfloat16, jnp.float32
     kept_shapes = (
-        ((SLOTS // 128, 128), jnp.int32), (patch, bf16), (patch, bf16), (patch, bf16), ((WIDTH, D), bf16),
+        ((SLOTS // 128, 128), jnp.int32), (patch, bf16), (patch, bf16), (patch, bf16), ((WIDTH, D), bf16), ((D, WIDTH), bf16),
         *(((HEADS_DEV, size, size), f32) for size in SIZES), (patch, f32),
     )
     send, *kept = pl.pallas_call(
         probs_kernel,
         out_shape=[pltpu.VMEM((PEERS, 2, IMG_DEV * WIDTH), bf16)] + [pltpu.VMEM(*s) for s in kept_shapes],
         in_specs=[anywhere] * 6,
-        out_specs=[here] * 10,
+        out_specs=[here] * 11,
         scratch_shapes=[
             pltpu.VMEM((IMG_DEV, WIDTH), bf16), pltpu.VMEM((ROWS, D), f32),
             pltpu.VMEM((3, max(SIZES), max(SIZES)), f32), pltpu.SemaphoreType.DMA((14,)),
@@ -252,10 +265,11 @@
     return pl.pallas_call(
         grads_kernel,
         out_shape=[jax.ShapeDtypeStruct((IMG_DEV, WIDTH), bf16)] + [grad_shape] * 3,
-        in_specs=[here] * 10,
+        in_specs=[here] * 11,
         out_specs=[anywhere] * 4,
         scratch_shapes=[pltpu.VMEM((IMG_DEV, WIDTH), bf16)] + [pltpu.VMEM(patch, bf16)] * 3
-        + [pltpu.VMEM((IMG_DEV, max(SIZES), max(SIZES)), bf16), pltpu.VMEM((ROWS, D), f32), pltpu.SemaphoreType.DMA((10,))],
+        + [pltpu.VMEM((IMG_DEV, max(SIZES), max(SIZES)), bf16), pltpu.VMEM((ROWS, D), f32), pltpu.VMEM((IMG_DEV, WIDTH), f32),
+           pltpu.SemaphoreType.DMA((10,))],
         compiler_params=pltpu.CompilerParams(vmem_limit_bytes=VMEM_LIMIT),
         name="grads",
     )(got, *kept)

time: 30.8 us -> 30.3 us (0.984)
  blocking collectives: 20.9 us -> 18.7 us
  Pallas kernels: 9.04 us -> 10.8 us
    pallas_call x1, Pallas kernels: 4.3 us -> 6.56 us  [on_device(): pl.pallas_call(probs_kernel, out_shape=[pltpu.VMEM((PEERS, 2, IMG_DEV * W...]
    all_to_all x1, blocking collectives: 20.9 us -> 18.7 us  [on_device(): got = lax.all_to_all(send, 'heads', 0, 0, tiled=False)]
    pallas_call x1, Pallas kernels: 4.74 us -> 4.27 us  [on_device(): pl.pallas_call(grads_kernel, out_shape=[jax.ShapeDtypeStruct((IMG_DEV, WI...]
where the time goes in v5:
time: 30.3 us; the launch traced here: 30.2 us
  blocking collectives  18.7 us (62%)
  Pallas kernels  10.8 us (36%)
  between operations  0.64 us (2%)
    all_to_all x1, blocking collectives, on_device(): got = lax.all_to_all(send, 'heads', 0, 0, tiled=False)  18.7 us
    pallas_call x1, Pallas kernels, on_device(): pl.pallas_call(probs_kernel, out_shape=[pltpu.VMEM((PEERS, 2, IMG_DEV * W...  6.56 us
    pallas_call x1, Pallas kernels, on_device(): pl.pallas_call(grads_kernel, out_shape=[jax.ShapeDtypeStruct((IMG_DEV, WI...  4.27 us

profile of v5, /device:TPU:1, one launch (start us, length us, event | category | flops | bytes accessed | tf_op | source)
XLA Modules:
  0.0 30.2 jit_solution(7057030730117703563)
XLA Ops:
  0.6 6.6 %probs.1 = (bf16[16,2,1152]{2,1,0:T(2,128)(2,1)S(1)}, s32[8,128]{1,0:T(8,128)S(1)}, bf16[1024,384]{1,0:T(8,128)(2,1)S(1)}, bf16[1024,384]{1,0:T(8,128)(2,1)S(1)}...) custom-call(s32[8,128]{1,0:T(8,128)} %bitcast.1, ...), custom_call_target="tpu_custom_call" | custom-call | tf_op jit(solution)/shard_map/probs/pallas_call | solution.py:251
  7.2 18.7 %all_to_all.5.got_ref = bf16[16,2,1152]{2,1,0:T(2,128)(2,1)S(1)} all-to-all(bf16[16,2,1152]{2,1,0:T(2,128)(2,1)S(1)} %get-tuple-element.15), channel_id=1, replica_groups=mesh['dp'=48,'heads'=16] {'heads'}, dimensions={0} | all-to-all | bytes 147456 | tf_op jit(solution)/shard_map/all_to_all | solution.py:263
  25.9 4.3 %grads.1 = (bf16[3,384]{1,0:T(4,128)(2,1)}, bf16[1024,384]{1,0:T(8,128)(2,1)}, bf16[1024,384]{1,0:T(8,128)(2,1)}, bf16[1024,384]{1,0:T(8,128)(2,1)}) custom-call(bf16[16,2,1152]{2,1,0:T(2,128)(2,1)S(1)} %all_to_all.5.got_ref, s32[8,128]{1,0:T(8,128)S(1)} %get-tuple-element.16.segment_ref, bf16[1024,384]{1,0:T(8,128)(2,1)S(1)} %get-tuple-element.17.q_ref, ...), custom_call_target="tpu_custom_call" | custom-call | tf_op jit(solution)/shard_map/grads/pallas_call | solution.py:265

commit v6 on v5

--- a/solution.py
+++ b/solution.py
@@ -114,9 +114,12 @@
         summed = jnp.sum(total * v_ref[rows, cols].astype(jnp.float32), axis=0, keepdims=True)
         means[image, head] = summed / jnp.maximum(live[image], 1).astype(jnp.float32)
 
-    def project(head):
-        mean = jnp.concatenate([means[image, head] for image in range(IMG_DEV)] + [jnp.zeros((5, HS), jnp.float32)], axis=0)
-        return dot(mean.astype(jnp.bfloat16), proj_ref[cols_of(head), :], NN)
+    def mean_of(head):
+        rows = [means[image, head] for image in range(IMG_DEV)] + [jnp.zeros((5, HS), jnp.float32)]
+        return jnp.concatenate(rows, axis=0).astype(jnp.bfloat16)
+
+    def project(head, span=slice(None)):
+        return dot(mean_of(head), proj_ref[cols_of(head), span], NN)
 
     means, slots = {}, {}
     arrive(("q", 0), ("k", 0))
@@ -134,25 +137,27 @@
     score(1, 1)
     unit(2, 0)
     score(2, 1)
-    arrive(("proj", 0))
-    share_ref[...] = project(0)
     unit(1, 1)
     score(1, 2)
     unit(2, 1)
     score(2, 2)
-    arrive(("proj", 1))
-    share_ref[...] += project(1)
+    arrive(("proj", 0), ("proj", 1))
+    both = jnp.concatenate([mean_of(0), mean_of(1)], axis=1)
+    share_ref[...] = dot(both, proj_ref[pl.ds(0, 2 * HS), :], NN)
     unit(1, 2)
     unit(2, 2)
     arrive(("proj", 2))
-    share_ref[...] += project(2)
     arrive("grad")
     grad = grad_ref[...].astype(jnp.float32)
     grad = jnp.concatenate([grad[image : image + 1] for image in range(IMG_DEV)], axis=1)
-    for peer in range(PEERS):
-        share = [share_ref[pl.ds(image, 1), pl.ds(peer * WIDTH, WIDTH)] for image in range(IMG_DEV)]
-        message = jnp.concatenate([jnp.concatenate(share, axis=1), grad], axis=0)
-        send_ref[peer] = message.astype(jnp.bfloat16)
+    peers = PEERS // 4
+    for part in range(4):
+        span = pl.ds(part * peers * WIDTH, peers * WIDTH)
+        share_ref[:, span] += project(2, span)
+        for peer in range(part * peers, (part + 1) * peers):
+            share = [share_ref[pl.ds(image, 1), pl.ds(peer * WIDTH, WIDTH)] for image in range(IMG_DEV)]
+            message = jnp.concatenate([jnp.concatenate(share, axis=1), grad], axis=0)
+            send_ref[peer] = message.astype(jnp.bfloat16)
 
     @pl.when(jnp.logical_not(enters_last()))
     def _():

time: 30.3 us -> 30.2 us (level)
  no operation moved by 1% of the time
where the time goes in v6:
time: 30.2 us; the launch traced here: 30.1 us
  blocking collectives  18.7 us (62%)
  Pallas kernels  10.8 us (36%)
  between operations  0.64 us (2%)
    all_to_all x1, blocking collectives, on_device(): got = lax.all_to_all(send, 'heads', 0, 0, tiled=False)  18.7 us
    pallas_call x1, Pallas kernels, on_device(): pl.pallas_call(probs_kernel, out_shape=[pltpu.VMEM((PEERS, 2, IMG_DEV * W...  6.48 us
    pallas_call x1, Pallas kernels, on_device(): pl.pallas_call(grads_kernel, out_shape=[jax.ShapeDtypeStruct((IMG_DEV, WI...  4.27 us

profile of v6, /device:TPU:1, one launch (start us, length us, event | category | flops | bytes accessed | tf_op | source)
XLA Modules:
  0.0 30.1 jit_solution(16486329118098497527)
XLA Ops:
  0.6 6.5 %probs.1 = (bf16[16,2,1152]{2,1,0:T(2,128)(2,1)S(1)}, s32[8,128]{1,0:T(8,128)S(1)}, bf16[1024,384]{1,0:T(8,128)(2,1)S(1)}, bf16[1024,384]{1,0:T(8,128)(2,1)S(1)}...) custom-call(s32[8,128]{1,0:T(8,128)} %bitcast.1, ...), custom_call_target="tpu_custom_call" | custom-call | tf_op jit(solution)/shard_map/probs/pallas_call | solution.py:256
  7.1 18.7 %all_to_all.5.got_ref = bf16[16,2,1152]{2,1,0:T(2,128)(2,1)S(1)} all-to-all(bf16[16,2,1152]{2,1,0:T(2,128)(2,1)S(1)} %get-tuple-element.15), channel_id=1, replica_groups=mesh['dp'=48,'heads'=16] {'heads'}, dimensions={0} | all-to-all | bytes 147456 | tf_op jit(solution)/shard_map/all_to_all | solution.py:268
  25.8 4.3 %grads.1 = (bf16[3,384]{1,0:T(4,128)(2,1)}, bf16[1024,384]{1,0:T(8,128)(2,1)}, bf16[1024,384]{1,0:T(8,128)(2,1)}, bf16[1024,384]{1,0:T(8,128)(2,1)}) custom-call(bf16[16,2,1152]{2,1,0:T(2,128)(2,1)S(1)} %all_to_all.5.got_ref, s32[8,128]{1,0:T(8,128)S(1)} %get-tuple-element.16.segment_ref, bf16[1024,384]{1,0:T(8,128)(2,1)S(1)} %get-tuple-element.17.q_ref, ...), custom_call_target="tpu_custom_call" | custom-call | tf_op jit(solution)/shard_map/grads/pallas_call | solution.py:270
